TPU v7x, 256 devices: a whole 4x4x8 slice. The times are simulated.
256 devices in a mesh: section: 8 (over z), expert: 16 (over y, x), dp: 2 (over core).
Axes of the slice: x: 4, y: 4, z: 8, core: 2. Of those that a mesh axis runs over, the one named last changes fastest.
Arguments:
- acts: bfloat16 [8, 3, 2048, 1024], P('section', None, ('expert', 'dp')), may hold values from -6 to 6
- out_grad: bfloat16 [3, 2048, 1024], P(None, ('expert', 'dp')), may hold values from -6 to 6
- ln_gain: float32 [8, 1024], P('section'), may hold values from 0.1 to 1.9
- router: bfloat16 [8, 1024, 16], P('section'), may hold values from -0.1875 to 0.1875
- w_in: bfloat16 [8, 16, 1024, 4096], P('section', 'expert', None, 'dp'), may hold values from -0.1875 to 0.1875
- w_out: bfloat16 [8, 16, 4096, 1024], P('section', 'expert', 'dp'), may hold values from -0.09375 to 0.09375
- expert_ids: int32 [8, 3, 2048, 2], P('section', None, ('expert', 'dp')), may hold values from 0 to 15, as said below
- slot_ids: int32 [8, 3, 2048, 2], P('section', None, ('expert', 'dp')), may hold values from 0 to 9, as said below
- capacity: int32 [8, 3, 16], P('section'), may hold values from 5 to 10
Outputs:
- in_grads: bfloat16 [8, 3, 2048, 1024], P('section', None, ('expert', 'dp'))
- gain_grad: float32 [8, 1024], P('section')
- router_grad: float32 [8, 1024, 16], P('section')
Inputs may be any that keep to these rules, and one draw needn't show every extreme that they name: `expert_ids`: A token's two experts differ. `slot_ids`: within one block, micro-batch and aligned block of 64 tokens (the tokens of one device), the choices that name one expert hold the slots 0, 1, 2, ... without gaps, at most 10 of them; in every block and micro-batch one expert has 10 choices from every aligned block and capacity 10.
All inputs are finite; a program needn't handle non-finite values.
Results may differ from a plain program's by a relative error of at most 0.03.
Values may be sent and summed in bfloat16 or wider, within the bound.
A program may use at most 128 MiB of HBM per device.

v0:
```python
import math

import jax
import jax.numpy as jnp
from jax import lax
from jax.sharding import PartitionSpec as P

GELU_C = math.sqrt(2.0 / math.pi)
PRECISE = lax.Precision.HIGHEST


def from_behind(shard, axis, by):
    count = lax.axis_size(axis)
    pairs = [(i, i + by) for i in range(count) if 0 <= i + by < count]
    return lax.ppermute(shard, axis, pairs)


def gelu_pair(hidden):
    inner_arg = GELU_C * (hidden + 0.044715 * hidden * hidden * hidden)
    tanh_val = jnp.tanh(inner_arg)
    active = 0.5 * hidden * (1.0 + tanh_val)
    gelu_slope = 0.5 * (1.0 + tanh_val) + 0.5 * hidden * (1.0 - tanh_val * tanh_val) * GELU_C * (
        1.0 + 3.0 * 0.044715 * hidden * hidden
    )
    return (active, gelu_slope)


def token_forward(inputs, norm_scale_weight, router_w):
    values = inputs.astype(jnp.float32)
    centred = values - jnp.mean(values, axis=-1, keepdims=True)
    inverse_deviation = lax.rsqrt(jnp.mean(centred * centred, axis=-1, keepdims=True) + 1e-06)
    expert_unit_rows = centred * inverse_deviation
    normed = (expert_unit_rows * norm_scale_weight).astype(jnp.bfloat16)
    logits = jnp.dot(normed, router_w, preferred_element_type=jnp.float32)
    return (expert_unit_rows, inverse_deviation, normed, logits)


def gate_pair(chosen):
    first_gate = 1.0 / (1.0 + jnp.exp(chosen[:, 1] - chosen[:, 0]))
    return jnp.stack([first_gate, 1.0 - first_gate], axis=1)


def token_backward(
    grad_out,
    expert_unit_rows,
    inverse_deviation,
    normed,
    norm_scale_weight,
    router_w,
    gate_vals,
    pick_table,
    gate_dots,
    expert_part,
):
    gate_diff = gate_vals[:, 0] * gate_vals[:, 1] * (gate_dots[:, 0] - gate_dots[:, 1])
    dlogits = gate_diff[:, None] * (pick_table[:, 0, :] - pick_table[:, 1, :])
    norm_gradient = expert_part + jnp.dot(
        dlogits, router_w.astype(jnp.float32).T, precision=PRECISE
    )
    router_term = jnp.dot(normed.astype(jnp.float32).T, dlogits, precision=PRECISE)
    gain_term = jnp.sum(norm_gradient * expert_unit_rows, axis=0)
    normalized_input_gradient = norm_gradient * norm_scale_weight
    input_gradient = inverse_deviation * (
        normalized_input_gradient
        - jnp.mean(normalized_input_gradient, axis=-1, keepdims=True)
        - expert_unit_rows
        * jnp.mean(normalized_input_gradient * expert_unit_rows, axis=-1, keepdims=True)
    )
    in_grad = (grad_out.astype(jnp.float32) + input_gradient).astype(jnp.bfloat16)
    return (in_grad, gain_term, router_term)


def expert_terms(rows_u, rows_grad, first_proj, second_proj):
    hidden = jnp.dot(rows_u, first_proj, preferred_element_type=jnp.float32)
    active, gelu_slope = gelu_pair(hidden)
    back_grad = lax.dot_general(
        rows_grad, second_proj, (((1,), (1,)), ((), ())), preferred_element_type=jnp.float32
    )
    gate_part = jnp.sum(active * back_grad, axis=-1)
    pre_grad = (back_grad * gelu_slope).astype(jnp.bfloat16)
    slot_part = lax.dot_general(
        pre_grad, first_proj, (((1,), (1,)), ((), ())), preferred_element_type=jnp.float32
    )
    return (slot_part, gate_part)


def per_device(acts, out_grad, ln_gain, router, w_in, w_out, expert_ids, slot_ids, capacity):
    section_count = lax.axis_size("section")
    section_index = lax.axis_index("section")
    microbatch_count = acts.shape[1]
    tok_rows = acts.shape[2]
    model_width = acts.shape[3]
    experts = router.shape[2]
    top_count = expert_ids.shape[3]
    cap_slots = 5 * tok_rows * top_count // (4 * experts)
    slot_count = experts * cap_slots
    tokens_all = tok_rows * lax.axis_size("expert") * lax.axis_size("dp")
    grad_scale = 1.0 / math.sqrt(microbatch_count * tokens_all)
    norm_scale_weight = ln_gain[0]
    router_w = router[0]
    first_proj = w_in[0, 0]
    second_proj = w_out[0, 0]
    positions = jnp.arange(slot_count, dtype=jnp.int32)
    columns = jnp.arange(experts, dtype=jnp.int32)
    section_acts = acts[0]
    section_ids = expert_ids[0]
    section_slots = slot_ids[0]
    section_caps = capacity[0]

    def run_experts(recv_u, recv_grad, is_valid):
        lead_rows = recv_u.shape[0]
        flat_u = recv_u.reshape(lead_rows * cap_slots, model_width)
        flat_grad = recv_grad.reshape(lead_rows * cap_slots, model_width)

        def expert_work(packed):
            return expert_terms(packed[0], packed[1], first_proj, second_proj)

        def skip_work(packed):
            return (
                jnp.zeros(packed[0].shape, jnp.float32),
                jnp.zeros(packed[0].shape[:1], jnp.float32),
            )

        slot_part, gate_part = lax.cond(is_valid, expert_work, skip_work, (flat_u, flat_grad))
        return (
            slot_part.reshape(lead_rows, cap_slots, model_width),
            gate_part.reshape(lead_rows, cap_slots),
        )

    def step_fn(step_index, loop_state):
        incoming, grads_acc, gain_acc, router_acc = loop_state
        micro_index = step_index - (section_count - 1 - section_index)
        is_valid = jnp.logical_and(micro_index >= 0, micro_index < microbatch_count)
        picked = jnp.clip(micro_index, 0, microbatch_count - 1)
        last_grad = lax.dynamic_index_in_dim(out_grad, picked, 0, keepdims=False)
        grad_out = jnp.where(section_index == section_count - 1, last_grad, incoming)
        inputs_now = lax.dynamic_index_in_dim(section_acts, picked, 0, keepdims=False)
        ids_now = lax.dynamic_index_in_dim(section_ids, picked, 0, keepdims=False)
        slots_now = lax.dynamic_index_in_dim(section_slots, picked, 0, keepdims=False)
        caps_now = lax.dynamic_index_in_dim(section_caps, picked, 0, keepdims=False)
        expert_unit_rows, inverse_deviation, normed, logits = token_forward(
            inputs_now, norm_scale_weight, router_w
        )
        pick_bool = ids_now[:, :, None] == columns
        pick_table = pick_bool.astype(jnp.float32)
        chosen = jnp.sum(pick_table * logits[:, None, :], axis=2)
        gate_vals = gate_pair(chosen)
        cap_sel = jnp.sum(jnp.where(pick_bool, caps_now, 0), axis=2)
        kept_mask = slots_now < cap_sel
        target = jnp.where(kept_mask, ids_now * cap_slots + slots_now, -1)
        send_map = jnp.any(positions[:, None, None] == target[None, :, :], axis=2).astype(
            jnp.bfloat16
        )
        sent_u = (
            jnp.dot(send_map, normed, preferred_element_type=jnp.float32)
            .astype(jnp.bfloat16)
            .reshape(experts, cap_slots, model_width)
        )
        sent_grad = (
            jnp.dot(send_map, grad_out, preferred_element_type=jnp.float32)
            .astype(jnp.bfloat16)
            .reshape(experts, cap_slots, model_width)
        )
        recv_u, recv_grad = (
            lax.all_to_all(sent_u, "expert", split_axis=0, concat_axis=0, tiled=True),
            lax.all_to_all(sent_grad, "expert", split_axis=0, concat_axis=0, tiled=True),
        )
        both_u, both_grad = (
            lax.all_gather(recv_u, "dp", axis=0, tiled=True),
            lax.all_gather(recv_grad, "dp", axis=0, tiled=True),
        )
        slot_part, gate_part = run_experts(both_u, both_grad, is_valid)
        summed_u, summed_g = (
            lax.psum_scatter(slot_part, "dp", scatter_dimension=0, tiled=True),
            lax.psum_scatter(gate_part, "dp", scatter_dimension=0, tiled=True),
        )
        ret_u, ret_g = (
            lax.all_to_all(
                summed_u.astype(jnp.bfloat16), "expert", split_axis=0, concat_axis=0, tiled=True
            ),
            lax.all_to_all(
                summed_g.astype(jnp.bfloat16), "expert", split_axis=0, concat_axis=0, tiled=True
            ),
        )
        flat_ret = ret_u.reshape(slot_count, model_width).astype(jnp.float32)
        flat_gate = ret_g.reshape(slot_count).astype(jnp.float32)
        hit_table = (target[:, :, None] == positions).astype(jnp.float32)
        mix_table = jnp.sum(hit_table * gate_vals[:, :, None], axis=1)
        expert_part = jnp.dot(mix_table, flat_ret, precision=PRECISE)
        gate_dots = jnp.sum(hit_table * flat_gate, axis=2)
        in_grad, gain_term, router_term = token_backward(
            grad_out,
            expert_unit_rows,
            inverse_deviation,
            normed,
            norm_scale_weight,
            router_w,
            gate_vals,
            pick_table,
            gate_dots,
            expert_part,
        )
        grads_acc = jnp.where(
            is_valid, lax.dynamic_update_index_in_dim(grads_acc, in_grad, picked, 0), grads_acc
        )
        gain_acc = gain_acc + jnp.where(is_valid, gain_term, 0.0)
        router_acc = router_acc + jnp.where(is_valid, router_term, 0.0)
        outgoing = from_behind(in_grad, "section", -1)
        return (outgoing, grads_acc, gain_acc, router_acc)

    start_state = (
        jnp.zeros((tok_rows, model_width), jnp.bfloat16),
        jnp.zeros((microbatch_count, tok_rows, model_width), jnp.bfloat16),
        jnp.zeros((model_width,), jnp.float32),
        jnp.zeros((model_width, experts), jnp.float32),
    )
    final_state = lax.fori_loop(0, microbatch_count + section_count - 1, step_fn, start_state)
    grads_acc = final_state[1]
    gain_acc, router_acc = (
        lax.psum(final_state[2].astype(jnp.bfloat16), ("expert", "dp")).astype(jnp.float32),
        lax.psum(final_state[3].astype(jnp.bfloat16), ("expert", "dp")).astype(jnp.float32),
    )
    return (grads_acc[None], (gain_acc * grad_scale)[None], (router_acc * grad_scale)[None])


def solution(mesh):
    return jax.shard_map(
        per_device,
        mesh=mesh,
        in_specs=(
            P("section", None, ("expert", "dp"), None),
            P(None, ("expert", "dp"), None),
            P("section", None),
            P("section", None, None),
            P("section", "expert", None, "dp"),
            P("section", "expert", "dp", None),
            P("section", None, ("expert", "dp"), None),
            P("section", None, ("expert", "dp"), None),
            P("section", None, None),
        ),
        out_specs=(
            P("section", None, ("expert", "dp"), None),
            P("section", None),
            P("section", None, None),
        ),
        check_vma=False,
    )
```

profile of v0, /device:TPU:1, one launch (start us, length us, event | category | flops | bytes accessed | tf_op | source)
XLA Modules:
  0.0 1211.0 jit_solution(11664580615775685706)
XLA Ops:
  7.9 1074.0 %while.23 = (s32[]{:T(128)}, bf16[64,1024]{1,0:T(8,128)(2,1)S(1)}, bf16[3,64,1024]{2,1,0:T(8,128)(2,1)S(1)}, f32[1024]{0:T(1024)S(1)}, f32[1024,16]{0,1:T(8,128)...) while((s32[]{:T(128)}, bf16[64,1024]{1,0:T(8,128)(2,1)S(1)}, ...), condition=%wide.region_16.17_spmd.clone.clone, body=%wide.region_0.16_spmd.clone.clone.sunk | while | flops 4244209152 | bytes 89025160 | solution.py:217
  22.7 9.3 all-to-all-done.1
  53.8 22.6 %reduce-scatter.3.cloned.1.call-done = f32[16,10]{1,0:T(8,128)} async-done(((f32[32,10]{1,0:T(8,128)}), f32[16,10]{1,0:T(8,128)}) %reduce-scatter.3.cloned.1.call-update) | async-done | bytes 656 | tf_op jit(solution)/shard_map/while/body/eval_jaxpr/reduce_scatter | solution.py:175
  104.0 10.2 all-to-all-done.3
  131.5 7.8 all-to-all-done.1
  162.5 20.9 %reduce-scatter.3.cloned.1.call-done = f32[16,10]{1,0:T(8,128)} async-done(((f32[32,10]{1,0:T(8,128)}), f32[16,10]{1,0:T(8,128)}) %reduce-scatter.3.cloned.1.call-update) | async-done | bytes 656 | tf_op jit(solution)/shard_map/while/body/eval_jaxpr/reduce_scatter | solution.py:175
  211.0 10.2 all-to-all-done.3
  238.4 7.8 all-to-all-done.1
  269.5 21.7 %reduce-scatter.3.cloned.1.call-done = f32[16,10]{1,0:T(8,128)} async-done(((f32[32,10]{1,0:T(8,128)}), f32[16,10]{1,0:T(8,128)}) %reduce-scatter.3.cloned.1.call-update) | async-done | bytes 656 | tf_op jit(solution)/shard_map/while/body/eval_jaxpr/reduce_scatter | solution.py:175
  318.7 10.3 all-to-all-done.3
  346.2 7.8 all-to-all-done.1
  377.2 22.5 %reduce-scatter.3.cloned.1.call-done = f32[16,10]{1,0:T(8,128)} async-done(((f32[32,10]{1,0:T(8,128)}), f32[16,10]{1,0:T(8,128)}) %reduce-scatter.3.cloned.1.call-update) | async-done | bytes 656 | tf_op jit(solution)/shard_map/while/body/eval_jaxpr/reduce_scatter | solution.py:175
  427.4 10.2 all-to-all-done.3
  454.9 7.8 all-to-all-done.1
  485.9 22.5 %reduce-scatter.3.cloned.1.call-done = f32[16,10]{1,0:T(8,128)} async-done(((f32[32,10]{1,0:T(8,128)}), f32[16,10]{1,0:T(8,128)}) %reduce-scatter.3.cloned.1.call-update) | async-done | bytes 656 | tf_op jit(solution)/shard_map/while/body/eval_jaxpr/reduce_scatter | solution.py:175
  535.9 10.2 all-to-all-done.3
  563.4 7.8 all-to-all-done.1
  594.4 22.5 %reduce-scatter.3.cloned.1.call-done = f32[16,10]{1,0:T(8,128)} async-done(((f32[32,10]{1,0:T(8,128)}), f32[16,10]{1,0:T(8,128)}) %reduce-scatter.3.cloned.1.call-update) | async-done | bytes 656 | tf_op jit(solution)/shard_map/while/body/eval_jaxpr/reduce_scatter | solution.py:175
  644.5 10.3 all-to-all-done.3
  672.0 7.8 all-to-all-done.1
  703.0 21.5 %reduce-scatter.3.cloned.1.call-done = f32[16,10]{1,0:T(8,128)} async-done(((f32[32,10]{1,0:T(8,128)}), f32[16,10]{1,0:T(8,128)}) %reduce-scatter.3.cloned.1.call-update) | async-done | bytes 656 | tf_op jit(solution)/shard_map/while/body/eval_jaxpr/reduce_scatter | solution.py:175
  752.1 10.3 all-to-all-done.3
  779.6 7.8 all-to-all-done.1
  807.0 14.4 %conditional.4 = (f32[320,1024]{1,0:T(8,128)S(1)}, f32[320]{0:T(512)S(1)}) conditional(s32[]{:T(128)} %convert_element_type.282, () %tuple.80, (bf16[32,10,1024]{2,0,1:T(8,128)(2,1)S(1)}, bf16[2048,1024]{1,0:T(8,128)(2,1)}, bf16[32,10,1024]{2,0,1:T(8,128)(2,1)S(1)}, bf16[1024,2048]{1,0:T(8,128)(2,1)}) %tuple.81), branch_computations={%region_7.7_spmd, %region_8.9_spmd} | conditional | flops 4045537024 | bytes 60818760 | solution.py:124
  857.4 10.3 all-to-all-done.3
  884.9 7.8 all-to-all-done.1
  912.4 14.4 %conditional.4 = (f32[320,1024]{1,0:T(8,128)S(1)}, f32[320]{0:T(512)S(1)}) conditional(s32[]{:T(128)} %convert_element_type.282, () %tuple.80, (bf16[32,10,1024]{2,0,1:T(8,128)(2,1)S(1)}, bf16[2048,1024]{1,0:T(8,128)(2,1)}, bf16[32,10,1024]{2,0,1:T(8,128)(2,1)S(1)}, bf16[1024,2048]{1,0:T(8,128)(2,1)}) %tuple.81), branch_computations={%region_7.7_spmd, %region_8.9_spmd} | conditional | flops 4045537024 | bytes 60818760 | solution.py:124
  961.8 10.3 all-to-all-done.3
  989.3 7.8 all-to-all-done.1
  1016.7 14.4 %conditional.4 = (f32[320,1024]{1,0:T(8,128)S(1)}, f32[320]{0:T(512)S(1)}) conditional(s32[]{:T(128)} %convert_element_type.282, () %tuple.80, (bf16[32,10,1024]{2,0,1:T(8,128)(2,1)S(1)}, bf16[2048,1024]{1,0:T(8,128)(2,1)}, bf16[32,10,1024]{2,0,1:T(8,128)(2,1)S(1)}, bf16[1024,2048]{1,0:T(8,128)(2,1)}) %tuple.81), branch_computations={%region_7.7_spmd, %region_8.9_spmd} | conditional | flops 4045537024 | bytes 60818760 | solution.py:124
  1065.2 10.3 all-to-all-done.3
  1082.0 121.0 %all-reduce = (bf16[1024]{0:T(1024)(128)(2,1)S(1)}, bf16[1024,16]{0,1:T(8,128)(2,1)S(1)}) all-reduce(bf16[1024]{0:T(1024)(128)(2,1)S(1)} %convert_element_type.153, bf16[1024,16]{0,1:T(8,128)(2,1)S(1)} %convert_element_type.155), channel_id=1, replica_groups=mesh['section'=8,'expert'=16,'dp'=2] {'expert','dp'}, use_global_device_ids=true, to_apply=%region_17.18 | all-reduce | flops 17408 | bytes 69632 | tf_op jit(solution)/shard_map/psum | solution.py:220
  (668 shorter events, 737.6 us)
Async XLA Ops:
  13.9 18.1 %all-to-all-start.1 = ((bf16[16,10,1024]{2,1,0:T(8,128)(2,1)}), bf16[16,10,1024]{2,1,0:T(8,128)(2,1)S(1)}, u32[]{:S(2)}, u32[]{:S(2)}) async-start(bf16[16,10,1024]{2,1,0:T(8,128)(2,1)} %reshape.239), calls=%async_computation.1 | async-start | bytes 1048576 | tf_op jit(solution)/shard_map/while/body/eval_jaxpr/all_to_all | solution.py:165
  32.0 13.2 %all-to-all-start = ((bf16[16,10,1024]{2,1,0:T(8,128)(2,1)}), bf16[16,10,1024]{2,1,0:T(8,128)(2,1)S(1)}, u32[]{:S(2)}, u32[]{:S(2)}) async-start(bf16[16,10,1024]{2,1,0:T(8,128)(2,1)} %reshape.238), calls=%async_computation | async-start | bytes 1048576 | tf_op jit(solution)/shard_map/while/body/eval_jaxpr/all_to_all | solution.py:166
  35.6 40.7 %reduce-scatter.3.cloned.1.call-start = ((), (), s32[]{:S(2)}) async-start(), calls=%async_computation.6 | async-start | bytes 24576 | tf_op jit(solution)/shard_map/while/body/eval_jaxpr/reduce_scatter | solution.py:175
  51.1 43.8 %reduce-scatter.5.cloned.1.call-start = ((), (), s32[]{:S(2)}) async-start(), calls=%async_computation.7 | async-start | bytes 3145728 | tf_op jit(solution)/shard_map/while/body/eval_jaxpr/reduce_scatter | solution.py:174
  97.0 17.2 %all-to-all-start.3 = ((bf16[16,10,1024]{2,1,0:T(8,128)(2,1)}), bf16[16,10,1024]{2,1,0:T(8,128)(2,1)S(1)}, u32[]{:S(2)}, u32[]{:S(2)}) async-start(bf16[16,10,1024]{2,1,0:T(8,128)(2,1)} %convert_element_type.283), calls=%async_computation.5 | async-start | bytes 1048576 | tf_op jit(solution)/shard_map/while/body/eval_jaxpr/all_to_all | solution.py:178
  142.9 40.6 %reduce-scatter.3.cloned.1.call-start = ((), (), s32[]{:S(2)}) async-start(), calls=%async_computation.6 | async-start | bytes 24576 | tf_op jit(solution)/shard_map/while/body/eval_jaxpr/reduce_scatter | solution.py:175
  159.9 42.0 %reduce-scatter.5.cloned.1.call-start = ((), (), s32[]{:S(2)}) async-start(), calls=%async_computation.7 | async-start | bytes 3145728 | tf_op jit(solution)/shard_map/while/body/eval_jaxpr/reduce_scatter | solution.py:174
  204.0 17.2 %all-to-all-start.3 = ((bf16[16,10,1024]{2,1,0:T(8,128)(2,1)}), bf16[16,10,1024]{2,1,0:T(8,128)(2,1)S(1)}, u32[]{:S(2)}, u32[]{:S(2)}) async-start(bf16[16,10,1024]{2,1,0:T(8,128)(2,1)} %convert_element_type.283), calls=%async_computation.5 | async-start | bytes 1048576 | tf_op jit(solution)/shard_map/while/body/eval_jaxpr/all_to_all | solution.py:178
  249.8 41.3 %reduce-scatter.3.cloned.1.call-start = ((), (), s32[]{:S(2)}) async-start(), calls=%async_computation.6 | async-start | bytes 24576 | tf_op jit(solution)/shard_map/while/body/eval_jaxpr/reduce_scatter | solution.py:175
  266.8 42.8 %reduce-scatter.5.cloned.1.call-start = ((), (), s32[]{:S(2)}) async-start(), calls=%async_computation.7 | async-start | bytes 3145728 | tf_op jit(solution)/shard_map/while/body/eval_jaxpr/reduce_scatter | solution.py:174
  311.7 17.3 %all-to-all-start.3 = ((bf16[16,10,1024]{2,1,0:T(8,128)(2,1)}), bf16[16,10,1024]{2,1,0:T(8,128)(2,1)S(1)}, u32[]{:S(2)}, u32[]{:S(2)}) async-start(bf16[16,10,1024]{2,1,0:T(8,128)(2,1)} %convert_element_type.283), calls=%async_computation.5 | async-start | bytes 1048576 | tf_op jit(solution)/shard_map/while/body/eval_jaxpr/all_to_all | solution.py:178
  357.6 42.1 %reduce-scatter.3.cloned.1.call-start = ((), (), s32[]{:S(2)}) async-start(), calls=%async_computation.6 | async-start | bytes 24576 | tf_op jit(solution)/shard_map/while/body/eval_jaxpr/reduce_scatter | solution.py:175
  374.5 43.8 %reduce-scatter.5.cloned.1.call-start = ((), (), s32[]{:S(2)}) async-start(), calls=%async_computation.7 | async-start | bytes 3145728 | tf_op jit(solution)/shard_map/while/body/eval_jaxpr/reduce_scatter | solution.py:174
  420.4 17.2 %all-to-all-start.3 = ((bf16[16,10,1024]{2,1,0:T(8,128)(2,1)}), bf16[16,10,1024]{2,1,0:T(8,128)(2,1)S(1)}, u32[]{:S(2)}, u32[]{:S(2)}) async-start(bf16[16,10,1024]{2,1,0:T(8,128)(2,1)} %convert_element_type.283), calls=%async_computation.5 | async-start | bytes 1048576 | tf_op jit(solution)/shard_map/while/body/eval_jaxpr/all_to_all | solution.py:178
  466.3 42.1 %reduce-scatter.3.cloned.1.call-start = ((), (), s32[]{:S(2)}) async-start(), calls=%async_computation.6 | async-start | bytes 24576 | tf_op jit(solution)/shard_map/while/body/eval_jaxpr/reduce_scatter | solution.py:175
  483.2 43.6 %reduce-scatter.5.cloned.1.call-start = ((), (), s32[]{:S(2)}) async-start(), calls=%async_computation.7 | async-start | bytes 3145728 | tf_op jit(solution)/shard_map/while/body/eval_jaxpr/reduce_scatter | solution.py:174
  529.0 17.2 %all-to-all-start.3 = ((bf16[16,10,1024]{2,1,0:T(8,128)(2,1)}), bf16[16,10,1024]{2,1,0:T(8,128)(2,1)S(1)}, u32[]{:S(2)}, u32[]{:S(2)}) async-start(bf16[16,10,1024]{2,1,0:T(8,128)(2,1)} %convert_element_type.283), calls=%async_computation.5 | async-start | bytes 1048576 | tf_op jit(solution)/shard_map/while/body/eval_jaxpr/all_to_all | solution.py:178
  574.8 42.2 %reduce-scatter.3.cloned.1.call-start = ((), (), s32[]{:S(2)}) async-start(), calls=%async_computation.6 | async-start | bytes 24576 | tf_op jit(solution)/shard_map/while/body/eval_jaxpr/reduce_scatter | solution.py:175
  591.8 43.6 %reduce-scatter.5.cloned.1.call-start = ((), (), s32[]{:S(2)}) async-start(), calls=%async_computation.7 | async-start | bytes 3145728 | tf_op jit(solution)/shard_map/while/body/eval_jaxpr/reduce_scatter | solution.py:174
  637.5 17.3 %all-to-all-start.3 = ((bf16[16,10,1024]{2,1,0:T(8,128)(2,1)}), bf16[16,10,1024]{2,1,0:T(8,128)(2,1)S(1)}, u32[]{:S(2)}, u32[]{:S(2)}) async-start(bf16[16,10,1024]{2,1,0:T(8,128)(2,1)} %convert_element_type.283), calls=%async_computation.5 | async-start | bytes 1048576 | tf_op jit(solution)/shard_map/while/body/eval_jaxpr/all_to_all | solution.py:178
  683.4 41.1 %reduce-scatter.3.cloned.1.call-start = ((), (), s32[]{:S(2)}) async-start(), calls=%async_computation.6 | async-start | bytes 24576 | tf_op jit(solution)/shard_map/while/body/eval_jaxpr/reduce_scatter | solution.py:175
  700.4 42.6 %reduce-scatter.5.cloned.1.call-start = ((), (), s32[]{:S(2)}) async-start(), calls=%async_computation.7 | async-start | bytes 3145728 | tf_op jit(solution)/shard_map/while/body/eval_jaxpr/reduce_scatter | solution.py:174
  745.1 17.3 %all-to-all-start.3 = ((bf16[16,10,1024]{2,1,0:T(8,128)(2,1)}), bf16[16,10,1024]{2,1,0:T(8,128)(2,1)S(1)}, u32[]{:S(2)}, u32[]{:S(2)}) async-start(bf16[16,10,1024]{2,1,0:T(8,128)(2,1)} %convert_element_type.283), calls=%async_computation.5 | async-start | bytes 1048576 | tf_op jit(solution)/shard_map/while/body/eval_jaxpr/all_to_all | solution.py:178
  791.0 38.9 %reduce-scatter.3.cloned.1.call-start = ((), (), s32[]{:S(2)}) async-start(), calls=%async_computation.6 | async-start | bytes 24576 | tf_op jit(solution)/shard_map/while/body/eval_jaxpr/reduce_scatter | solution.py:175
  822.1 26.2 %reduce-scatter.5.cloned.1.call-start = ((), (), s32[]{:S(2)}) async-start(), calls=%async_computation.7 | async-start | bytes 3145728 | tf_op jit(solution)/shard_map/while/body/eval_jaxpr/reduce_scatter | solution.py:174
  850.4 17.3 %all-to-all-start.3 = ((bf16[16,10,1024]{2,1,0:T(8,128)(2,1)}), bf16[16,10,1024]{2,1,0:T(8,128)(2,1)S(1)}, u32[]{:S(2)}, u32[]{:S(2)}) async-start(bf16[16,10,1024]{2,1,0:T(8,128)(2,1)} %convert_element_type.283), calls=%async_computation.5 | async-start | bytes 1048576 | tf_op jit(solution)/shard_map/while/body/eval_jaxpr/all_to_all | solution.py:178
  896.3 37.9 %reduce-scatter.3.cloned.1.call-start = ((), (), s32[]{:S(2)}) async-start(), calls=%async_computation.6 | async-start | bytes 24576 | tf_op jit(solution)/shard_map/while/body/eval_jaxpr/reduce_scatter | solution.py:175
  927.5 25.2 %reduce-scatter.5.cloned.1.call-start = ((), (), s32[]{:S(2)}) async-start(), calls=%async_computation.7 | async-start | bytes 3145728 | tf_op jit(solution)/shard_map/while/body/eval_jaxpr/reduce_scatter | solution.py:174
  954.8 17.3 %all-to-all-start.3 = ((bf16[16,10,1024]{2,1,0:T(8,128)(2,1)}), bf16[16,10,1024]{2,1,0:T(8,128)(2,1)S(1)}, u32[]{:S(2)}, u32[]{:S(2)}) async-start(bf16[16,10,1024]{2,1,0:T(8,128)(2,1)} %convert_element_type.283), calls=%async_computation.5 | async-start | bytes 1048576 | tf_op jit(solution)/shard_map/while/body/eval_jaxpr/all_to_all | solution.py:178
  1000.7 36.9 %reduce-scatter.3.cloned.1.call-start = ((), (), s32[]{:S(2)}) async-start(), calls=%async_computation.6 | async-start | bytes 24576 | tf_op jit(solution)/shard_map/while/body/eval_jaxpr/reduce_scatter | solution.py:175
  1031.8 24.2 %reduce-scatter.5.cloned.1.call-start = ((), (), s32[]{:S(2)}) async-start(), calls=%async_computation.7 | async-start | bytes 3145728 | tf_op jit(solution)/shard_map/while/body/eval_jaxpr/reduce_scatter | solution.py:174
  1058.2 17.3 %all-to-all-start.3 = ((bf16[16,10,1024]{2,1,0:T(8,128)(2,1)}), bf16[16,10,1024]{2,1,0:T(8,128)(2,1)S(1)}, u32[]{:S(2)}, u32[]{:S(2)}) async-start(bf16[16,10,1024]{2,1,0:T(8,128)(2,1)} %convert_element_type.283), calls=%async_computation.5 | async-start | bytes 1048576 | tf_op jit(solution)/shard_map/while/body/eval_jaxpr/all_to_all | solution.py:178
  (85 other events, 713.3 us)
Sparse Core Ops, SparseCore 0:
  51.2 25.0 reduce-scatter.2
  78.8 16.0 reduce-scatter.4
  160.0 23.3 reduce-scatter.2
  185.8 16.0 reduce-scatter.4
  266.9 24.1 reduce-scatter.2
  293.5 16.0 reduce-scatter.4
  374.7 24.9 reduce-scatter.2
  402.2 16.0 reduce-scatter.4
  483.4 24.9 reduce-scatter.2
  510.7 16.0 reduce-scatter.4
  591.9 24.9 reduce-scatter.2
  619.3 16.0 reduce-scatter.4
  700.5 23.9 reduce-scatter.2
  726.9 16.0 reduce-scatter.4
  822.3 7.5 reduce-scatter.2
  832.2 16.0 reduce-scatter.4
  927.6 6.5 reduce-scatter.2
  936.6 16.0 reduce-scatter.4
  1032.0 5.6 reduce-scatter.2
  1040.0 16.0 reduce-scatter.4
where the time goes:
time: 1220 us; the launch traced here: 1210 us
  waiting for transfers between devices  533 us (44%)
  blocking collectives  241 us (20%)
  starting transfers between devices  216 us (18%)
  other arithmetic  71 us (6%)
  matrix products  66.8 us (5%)
  local copies, waits for them, and re-layouts  65.6 us (5%)
  between operations  14.1 us (1%)
    reduce_scatter x10, waiting for transfers between devices, step_fn(): lax.psum_scatter(gate_part, 'dp', scatter_dimension=0, tiled=True)  166 us
    psum x1, blocking collectives, per_device(): lax.psum(final_state[2].astype(jnp.bfloat16), ('expert', 'dp'))  121 us
    all_to_all x10, waiting for transfers between devices, step_fn(): lax.all_to_all(summed_u.astype(jnp.bfloat16), 'expert', split_axis=0, con...  103 us
    all_to_all x10, waiting for transfers between devices, step_fn(): lax.all_to_all(sent_u, 'expert', split_axis=0, concat_axis=0, tiled=True)  79.6 us
    all_gather x10, blocking collectives, step_fn(): lax.all_gather(recv_grad, 'dp', axis=0, tiled=True)  64.3 us
    all_to_all x10, starting transfers between devices, step_fn(): lax.all_to_all(summed_u.astype(jnp.bfloat16), 'expert', split_axis=0, con...  64 us
    all_to_all x10, waiting for transfers between devices, step_fn(): lax.all_to_all(summed_g.astype(jnp.bfloat16), 'expert', split_axis=0, con...  63.1 us
    all_to_all x10, starting transfers between devices, step_fn(): lax.all_to_all(summed_g.astype(jnp.bfloat16), 'expert', split_axis=0, con...  62.7 us
  transfers between devices with their start and end apart: 70, of which 70 were waited for; matrix products, arithmetic and copies ran while one was open for 5% of the time, Pallas kernels for 0%

commit v1 on v0

v1 whole, which is shorter than its diff:
```python
import functools
import math

import jax
import jax.numpy as jnp
from jax import lax
from jax.experimental import pallas as pl
from jax.experimental.pallas import tpu as pltpu
from jax.sharding import PartitionSpec as P

GELU_C = math.sqrt(2.0 / math.pi)
MESH = pl.DeviceIdType.MESH
BF = jnp.bfloat16
F32 = jnp.float32
SIDE = 4
LANES = 128


def plane_offsets():
    offs = [(k // SIDE, k % SIDE) for k in range(1, SIDE * SIDE)]
    far = lambda o: min(o[0], SIDE - o[0]) + min(o[1], SIDE - o[1])
    return sorted(offs, key=lambda o: -far(o))


def dot(a, b, ca=1, cb=0):
    return lax.dot_general(a, b, (((ca,), (cb,)), ((), ())), preferred_element_type=F32)


def iota(shape, dim):
    return lax.broadcasted_iota(jnp.int32, shape, dim)


def stack_chunks(x):
    return jnp.concatenate([x[:, c : c + LANES] for c in range(0, x.shape[1], LANES)], axis=0)


def spread_chunks(x, rows):
    return jnp.concatenate([x[r : r + rows] for r in range(0, x.shape[0], rows)], axis=1)


def kernel(
    acts, out_grad, gain, router_t, ids, codes, w_in_own, w_out_own,
    o_grads, o_gain, o_router,
    w_in, w_out, w_out_t, slope, active, pre, rows,
    su, ru, sy, ry, sg, rg, sr, rr, rz, sz,
    unit_s, inv_s, normed_s, ydiff_s, extra_s, pdg_s,
    send_main, send_tail, mix_main, mix_tail, diff_main, diff_tail,
    router_pad, perm, perm_t, eye, router_acc, gain_acc,
    fin_s, fin_r, fin_x, fin_y, fin_t, fin_g,
    w_local, w_send, w_recv,
    u_send, u_recv, y_send, y_recv, g_send, g_recv, r_send, r_recv, z_send, z_recv,
    f_send, f_recv,
    *, scale,
):
    sec = lax.axis_index("section")
    exp = lax.axis_index("expert")
    core = lax.axis_index("dp")
    sections = lax.axis_size("section")
    last = sections - 1
    col = exp // SIDE
    row = lax.rem(exp, SIDE)
    peers = [
        lax.rem(col + dy, SIDE) * SIDE + lax.rem(row + dx, SIDE) for dy, dx in plane_offsets()
    ]
    experts = SIDE * SIDE
    micros = acts.shape[0]
    toks = acts.shape[1]
    width = acts.shape[2]
    half = w_in_own.shape[1]

    own_in = pltpu.make_async_copy(w_in_own, w_in.at[:, pl.ds(0, half)], w_local.at[0])
    own_out = pltpu.make_async_copy(w_out_own, w_out.at[pl.ds(0, half), :], w_local.at[1])
    own_in.start()
    own_out.start()

    barrier = pltpu.get_barrier_semaphore()
    for p in peers:
        pl.semaphore_signal(barrier, inc=1, device_id=(sec, p, core), device_id_type=MESH)
    pl.semaphore_signal(barrier, inc=1, device_id=(sec, exp, 1 - core), device_id_type=MESH)

    @pl.when(sec < last)
    def _():
        pl.semaphore_signal(barrier, inc=1, device_id=(sec + 1, exp, core), device_id_type=MESH)

    @pl.when(sec > 0)
    def _():
        pl.semaphore_wait(barrier, experts + 1)

    @pl.when(sec == 0)
    def _():
        pl.semaphore_wait(barrier, experts)

    part_in = pltpu.make_async_remote_copy(
        src_ref=w_in_own, dst_ref=w_in.at[:, pl.ds(half, half)],
        send_sem=w_send.at[0], recv_sem=w_recv.at[0],
        device_id=(sec, exp, 1 - core), device_id_type=MESH,
    )
    part_out = pltpu.make_async_remote_copy(
        src_ref=w_out_own, dst_ref=w_out.at[pl.ds(half, half), :],
        send_sem=w_send.at[1], recv_sem=w_recv.at[1],
        device_id=(sec, exp, 1 - core), device_id_type=MESH,
    )
    part_in.start()
    part_out.start()

    def scatter(src, dst, m, send_sem, recv_sem):
        for p in peers:
            pltpu.make_async_remote_copy(
                src_ref=src.at[m, p], dst_ref=dst.at[m, exp],
                send_sem=send_sem.at[m], recv_sem=recv_sem.at[m],
                device_id=(sec, p, core), device_id_type=MESH,
            ).start()
        dst[m, exp] = src[m, exp]

    def all_of(buf, m, sem):
        part = buf.at[m, pl.ds(0, experts - 1)]
        return pltpu.make_async_copy(part, part, sem.at[m])

    def pack(buf, m, main, tail):
        main = main.reshape(experts, 8, width)
        for q in range(4):
            lo = main[:, :, 256 * q : 256 * q + LANES]
            hi = main[:, :, 256 * q + LANES : 256 * q + 256]
            buf[m, :, 16 * q : 16 * q + 16, :] = jnp.concatenate([lo, hi], axis=1).astype(BF)
        buf[m, :, 64:80, :] = tail.reshape(experts, 16, LANES).astype(BF)

    def unpack_main(buf, m):
        parts = []
        for q in range(4):
            t = buf[m, :, 16 * q : 16 * q + 16, :].astype(F32)
            parts.append(t[:, :8, :].reshape(experts * 8, LANES))
            parts.append(t[:, 8:, :].reshape(experts * 8, LANES))
        return jnp.concatenate(parts, axis=1).astype(BF)

    def tail_of(buf, m):
        return buf[m, :, 64:80, :].reshape(experts * 16, LANES)

    def to_slots(x, m, buf):
        pack(buf, m, dot(send_main[m], x), dot(send_tail[m], stack_chunks(x)))

    def to_rows(buf, m):
        rows[0 : experts * 8, :] = unpack_main(buf, m)
        t = dot(perm[...], tail_of(buf, m))
        rows[experts * 8 : experts * 10, :] = spread_chunks(t, experts * 2).astype(BF)

    def from_rows(res, m, buf):
        tail = stack_chunks(res[experts * 8 : experts * 10].astype(BF))
        pack(buf, m, res[0 : experts * 8], dot(perm_t[...], tail))

    def combine(buf, m, main_table, tail_table):
        main = dot(main_table[m], unpack_main(buf, m))
        tail = dot(tail_table[m], tail_of(buf, m))
        return main + spread_chunks(tail, toks)

    q = iota((256, 256), 0)
    r = iota((256, 256), 1)
    picked = ((q & 31) >> 1) * 16 + (q & 1) * 8 + (q >> 5)
    perm[...] = (r == picked).astype(F32).astype(BF)
    picked_t = ((r & 31) >> 1) * 16 + (r & 1) * 8 + (r >> 5)
    perm_t[...] = (q == picked_t).astype(F32).astype(BF)
    eye[...] = (q == r).astype(F32).astype(BF)
    router_pad[...] = jnp.zeros_like(router_pad)
    router_pad[0:experts, :] = router_t[...]
    router_acc[...] = jnp.zeros_like(router_acc)
    gain_acc[...] = jnp.zeros_like(gain_acc)

    def tokens_forward(m):
        x = acts[m].astype(F32)
        centred = x - jnp.mean(x, axis=-1, keepdims=True)
        inv = lax.rsqrt(jnp.mean(centred * centred, axis=-1, keepdims=True) + 1e-06)
        unit = centred * inv
        normed = (unit * gain[...]).astype(BF)
        unit_s[m] = unit
        inv_s[m] = jnp.broadcast_to(inv, (toks, LANES))
        normed_s[m] = normed
        code1 = codes[m, 0:1, :]
        code2 = codes[m, 1:2, :]
        slot_r = iota((128, LANES), 0)
        slot_code = (slot_r >> 3) * 16 + (slot_r & 7)
        hit = ((slot_code == code1) | (slot_code == code2)).astype(F32)
        send_main[m] = hit[:, :toks].astype(BF)
        wide1 = jnp.concatenate([code1] * 4, axis=1)
        wide2 = jnp.concatenate([code2] * 4, axis=1)
        tail_r = iota((256, 512), 0)
        tail_code = (tail_r >> 4) * 16 + 8 + ((tail_r >> 3) & 1)
        same = (iota((256, 512), 1) >> 6) == (tail_r & 7)
        hit = (((tail_code == wide1) | (tail_code == wide2)) & same).astype(F32)
        send_tail[m] = hit.astype(BF)
        to_slots(normed, m, su)
        scatter(su, ru, m, u_send, u_recv)
        logits = dot(router_t[...], jnp.concatenate([normed, normed], axis=0), 1, 1)
        id1 = ids[m, 0:1, :]
        id2 = ids[m, 1:2, :]
        e_r = iota((experts, LANES), 0)
        chosen1 = jnp.sum(jnp.where(e_r == id1, logits, 0.0), axis=0, keepdims=True)
        chosen2 = jnp.sum(jnp.where(e_r == id2, logits, 0.0), axis=0, keepdims=True)
        gate1 = 1.0 / (1.0 + jnp.exp(chosen2 - chosen1))
        gate2 = 1.0 - gate1
        line = iota((8, LANES), 0)
        lines = jnp.where(line == 0, code1.astype(F32), 0.0)
        lines = jnp.where(line == 1, code2.astype(F32), lines)
        lines = jnp.where(line == 2, id1.astype(F32), lines)
        lines = jnp.where(line == 3, id2.astype(F32), lines)
        lines = jnp.where(line == 4, gate1, lines)
        lines = jnp.where(line == 5, gate2, lines)
        lines = jnp.concatenate([lines, jnp.zeros((LANES - 8, LANES), F32)], axis=0)
        turned = jnp.transpose(lines)[:toks]
        c1 = turned[:, 0:1].astype(jnp.int32)
        c2 = turned[:, 1:2].astype(jnp.int32)
        i1 = turned[:, 2:3].astype(jnp.int32)
        i2 = turned[:, 3:4].astype(jnp.int32)
        g1 = turned[:, 4:5]
        g2 = turned[:, 5:6]
        e_l = iota((toks, LANES), 1)
        pdg_s[m] = g1 * g2 * ((e_l == i1).astype(F32) - (e_l == i2).astype(F32))
        slot_code = (e_l >> 3) * 16 + (e_l & 7)
        hit1 = (slot_code == c1).astype(F32)
        hit2 = (slot_code == c2).astype(F32)
        mix_main[m] = (g1 * hit1 + g2 * hit2).astype(BF)
        diff_main[m] = (hit1 - hit2).astype(BF)
        lane = iota((toks, 256), 1)
        tail_code = (lane >> 4) * 16 + 8 + ((lane >> 3) & 1)
        hit1 = (tail_code == c1).astype(F32)
        hit2 = (tail_code == c2).astype(F32)
        mixed = g1 * hit1 + g2 * hit2
        differ = hit1 - hit2
        for c in range(8):
            here = (lane & 7) == c
            mix_tail[m, toks * c : toks * c + toks, :] = jnp.where(here, mixed, 0.0).astype(BF)
            diff_tail[m, toks * c : toks * c + toks, :] = jnp.where(here, differ, 0.0).astype(BF)

    def experts_forward(m):
        all_of(ru, m, u_recv).wait()
        to_rows(ru, m)

        @pl.loop(0, 4)
        def _(n):
            cols = pl.ds(pl.multiple_of(n * 1024, 1024), 1024)
            hidden = dot(rows[...], w_in[:, cols])
            square = hidden * hidden
            tanh = jnp.tanh(GELU_C * hidden * (1.0 + 0.044715 * square))
            rise = 0.5 * (1.0 + tanh)
            active[:, cols] = (hidden * rise).astype(BF)
            bend = 0.5 * hidden * (1.0 - tanh * tanh) * (GELU_C + (3.0 * 0.044715 * GELU_C) * square)
            slope[m, :, cols] = (rise + bend).astype(BF)

    def experts_value(m):
        from_rows(dot(active[...], w_out[...]), m, sy)
        scatter(sy, ry, m, y_send, y_recv)

    def tokens_value(m):
        all_of(ry, m, y_recv).wait()
        ydiff_s[m] = combine(ry, m, diff_main, diff_tail)

    def tokens_send(m):
        to_slots(rz[m], m, sg)
        scatter(sg, rg, m, g_send, g_recv)

    def tokens_gate(m):
        dots = jnp.sum(ydiff_s[m] * rz[m].astype(F32), axis=1, keepdims=True)
        dlogits = (dots * pdg_s[m]).astype(BF)
        extra_s[...] = dot(dlogits, router_pad[...])
        router_acc[...] += dot(dlogits, normed_s[m], 0, 0)[:experts]

    def experts_backward(m, turned):
        all_of(rg, m, g_recv).wait()
        to_rows(rg, m)
        if turned:
            back = dot(rows[...], w_out_t[...])
        else:
            back = dot(rows[...], w_out[...], 1, 1)
        pre[...] = (back * slope[m].astype(F32)).astype(BF)
        if turned:
            res = dot(pre[...], w_out[...])
        else:
            res = dot(pre[...], w_in[...], 1, 1)
        from_rows(res, m, sr)
        scatter(sr, rr, m, r_send, r_recv)

    def tokens_backward(m):
        all_of(rr, m, r_recv).wait()
        unit = unit_s[m]
        norm_grad = combine(rr, m, mix_main, mix_tail) + extra_s[...]
        xhat = norm_grad * gain[...]
        mean1 = jnp.mean(xhat, axis=-1, keepdims=True)
        mean2 = jnp.mean(xhat * unit, axis=-1, keepdims=True)
        step = inv_s[m][:, 0:1] * (xhat - mean1 - unit * mean2)
        in_grad = (rz[m].astype(F32) + step).astype(BF)
        sz[m] = in_grad

        @pl.when(sec > 0)
        def _():
            z_copy(m).start()

        o_grads[m] = in_grad
        terms = (norm_grad * unit).reshape(toks // 8, 8, width)
        gain_acc[...] += jnp.sum(terms, axis=0)

    def z_copy(m):
        return pltpu.make_async_remote_copy(
            src_ref=sz.at[m], dst_ref=rz.at[m],
            send_sem=z_send.at[m], recv_sem=z_recv.at[m],
            device_id=(jnp.maximum(sec - 1, 0), exp, core), device_id_type=MESH,
        )

    @pl.when(sec == last)
    def _():
        @pl.loop(0, micros)
        def _(m):
            rz[m] = out_grad[m]
            tokens_forward(m)
            tokens_send(m)

            @pl.when(m == 0)
            def _():
                own_in.wait()
                part_in.wait_recv()

            experts_forward(m)

            @pl.when(m == 0)
            def _():
                own_out.wait()
                part_out.wait_recv()

            experts_value(m)
            experts_backward(m, False)
            tokens_value(m)
            tokens_gate(m)
            tokens_backward(m)

    @pl.when(sec < last)
    def _():
        pl.loop(0, micros)(tokens_forward)
        own_in.wait()
        part_in.wait_recv()
        own_out.wait()
        part_out.wait_recv()

        @pl.loop(0, micros)
        def _(m):
            experts_forward(m)
            experts_value(m)

        @pl.loop(0, width // 256)
        def _(n):
            lines = pl.ds(pl.multiple_of(n * 256, 256), 256)
            w_out_t[lines, :] = dot(eye[...], w_out[:, lines], 1, 1).astype(BF)

        @pl.loop(0, 2 * half // 256)
        def _(n):
            lines = pl.ds(pl.multiple_of(n * 256, 256), 256)
            w_out[lines, :] = dot(eye[...], w_in[:, lines], 1, 1).astype(BF)

        pl.loop(0, micros)(tokens_value)

        @pl.loop(0, micros)
        def _(m):
            z_copy(m).wait_recv()
            tokens_send(m)
            tokens_gate(m)
            experts_backward(m, True)
            tokens_backward(m)

    for j in range(experts):
        lines = slice(8 * (j // 8), 8 * (j // 8) + 8)
        cols = slice(LANES * (j % 8), LANES * (j % 8) + LANES)
        fin_s[0, j, 0:8, :] = router_acc[lines, cols]
        fin_s[0, j, 8:16, :] = gain_acc[:, cols] if j < 8 else jnp.zeros((8, LANES), F32)
    for p in peers:
        pltpu.make_async_remote_copy(
            src_ref=fin_s.at[0, p], dst_ref=fin_r.at[0, exp],
            send_sem=f_send.at[0], recv_sem=f_recv.at[0],
            device_id=(sec, p, core), device_id_type=MESH,
        ).start()
    fin_r[0, exp] = fin_s[0, exp]
    all_of(fin_r, 0, f_recv).wait()
    fin_x[...] = jnp.sum(fin_r[0], axis=0)
    pair = pltpu.make_async_remote_copy(
        src_ref=fin_x, dst_ref=fin_y, send_sem=f_send.at[1], recv_sem=f_recv.at[1],
        device_id=(sec, exp, 1 - core), device_id_type=MESH,
    )
    pair.start()
    pair.wait()
    fin_t[...] = (fin_x[...] + fin_y[...]) * scale
    for p in peers:
        pltpu.make_async_remote_copy(
            src_ref=fin_t, dst_ref=fin_g.at[0, exp],
            send_sem=f_send.at[2], recv_sem=f_recv.at[2],
            device_id=(sec, p, core), device_id_type=MESH,
        ).start()
    fin_g[0, exp] = fin_t[...]
    got = fin_g.at[0, pl.ds(0, experts - 1)]
    pltpu.make_async_copy(got, got, f_recv.at[2]).wait()
    for j in range(experts):
        lines = slice(8 * (j // 8), 8 * (j // 8) + 8)
        cols = slice(LANES * (j % 8), LANES * (j % 8) + LANES)
        o_router[lines, cols] = fin_g[0, j, 0:8, :]
        if j < 8:
            o_gain[:, cols] = jnp.sum(fin_g[0, j, 8:16, :], axis=0, keepdims=True)

    @pl.loop(0, micros)
    def _(m):
        all_of(su, m, u_send).wait()
        all_of(sy, m, y_send).wait()
        all_of(sg, m, g_send).wait()
        all_of(sr, m, r_send).wait()

        @pl.when(sec > 0)
        def _():
            z_copy(m).wait_send()

    all_of(fin_s, 0, f_send).wait()
    pltpu.make_async_copy(got, got, f_send.at[2]).wait()
    part_in.wait_send()
    part_out.wait_send()


def per_device(acts, out_grad, ln_gain, router, w_in, w_out, expert_ids, slot_ids, capacity):
    _, micros, toks, width = acts.shape
    experts = router.shape[2]
    half = w_in.shape[3]
    cap_slots = 10
    slots = experts * cap_slots
    tokens_all = toks * lax.axis_size("expert") * lax.axis_size("dp")
    scale = 1.0 / math.sqrt(micros * tokens_all)
    ids = jnp.transpose(expert_ids[0], (0, 2, 1))
    places = jnp.transpose(slot_ids[0], (0, 2, 1))
    columns = jnp.arange(experts, dtype=jnp.int32)
    caps = jnp.sum(
        jnp.where(ids[..., None] == columns, capacity[0][:, None, None, :], 0), axis=-1
    )
    codes = jnp.where(places < caps, ids * 16 + places, -1)
    codes = jnp.concatenate([codes, codes], axis=2)
    ids = jnp.concatenate([ids, ids], axis=2)
    vmem = pl.BlockSpec(memory_space=pltpu.VMEM)
    hbm = pl.BlockSpec(memory_space=pl.ANY)
    dma = pltpu.SemaphoreType.DMA
    tiles = (micros, experts, 80, LANES)
    grads, gain_out, router_out = pl.pallas_call(
        functools.partial(kernel, scale=scale),
        out_shape=(
            jax.ShapeDtypeStruct((micros, toks, width), BF),
            jax.ShapeDtypeStruct((1, width), F32),
            jax.ShapeDtypeStruct((experts, width), F32),
        ),
        in_specs=[vmem] * 6 + [hbm] * 2,
        out_specs=(vmem, vmem, vmem),
        scratch_shapes=[
            pltpu.VMEM((width, 2 * half), BF),
            pltpu.VMEM((2 * half, width), BF),
            pltpu.VMEM((width, 2 * half), BF),
            pltpu.VMEM((micros, slots, 2 * half), BF),
            pltpu.VMEM((slots, 2 * half), BF),
            pltpu.VMEM((slots, 2 * half), BF),
            pltpu.VMEM((slots, width), BF),
        ]
        + [pltpu.VMEM(tiles, BF)] * 8
        + [pltpu.VMEM((micros, toks, width), BF)] * 2
        + [
            pltpu.VMEM((micros, toks, width), F32),
            pltpu.VMEM((micros, toks, LANES), F32),
            pltpu.VMEM((micros, toks, width), BF),
            pltpu.VMEM((micros, toks, width), F32),
            pltpu.VMEM((toks, width), F32),
            pltpu.VMEM((micros, toks, LANES), F32),
            pltpu.VMEM((micros, 128, toks), BF),
            pltpu.VMEM((micros, 256, 512), BF),
            pltpu.VMEM((micros, toks, 128), BF),
            pltpu.VMEM((micros, 512, 256), BF),
            pltpu.VMEM((micros, toks, 128), BF),
            pltpu.VMEM((micros, 512, 256), BF),
            pltpu.VMEM((LANES, width), BF),
            pltpu.VMEM((256, 256), BF),
            pltpu.VMEM((256, 256), BF),
            pltpu.VMEM((256, 256), BF),
            pltpu.VMEM((experts, width), F32),
            pltpu.VMEM((8, width), F32),
            pltpu.VMEM((1, experts, 16, LANES), F32),
            pltpu.VMEM((1, experts, 16, LANES), F32),
            pltpu.VMEM((16, LANES), F32),
            pltpu.VMEM((16, LANES), F32),
            pltpu.VMEM((16, LANES), F32),
            pltpu.VMEM((1, experts, 16, LANES), F32),
            dma((2,)),
            dma((2,)),
            dma((2,)),
        ]
        + [dma((micros,))] * 10
        + [dma((3,))] * 2,
        compiler_params=pltpu.CompilerParams(
            collective_id=0, has_side_effects=True, vmem_limit_bytes=60 * 2**20
        ),
    )(
        acts[0],
        out_grad,
        ln_gain,
        jnp.transpose(router[0]),
        ids,
        codes,
        w_in[0, 0],
        w_out[0, 0],
    )
    return (grads[None], gain_out, jnp.transpose(router_out)[None])


def solution(mesh):
    return jax.shard_map(
        per_device,
        mesh=mesh,
        in_specs=(
            P("section", None, ("expert", "dp"), None),
            P(None, ("expert", "dp"), None),
            P("section", None),
            P("section", None, None),
            P("section", "expert", None, "dp"),
            P("section", "expert", "dp", None),
            P("section", None, ("expert", "dp"), None),
            P("section", None, ("expert", "dp"), None),
            P("section", None, None),
        ),
        out_specs=(
            P("section", None, ("expert", "dp"), None),
            P("section", None),
            P("section", None, None),
        ),
        check_vma=False,
    )
```

time: 1220 us -> 243 us (0.20)
  waiting for transfers between devices: 533 us -> 0 us
  blocking collectives: 241 us -> 0 us
  Pallas kernels: 0 us -> 234 us
  starting transfers between devices: 216 us -> 0 us
  other arithmetic: 71 us -> 2.9 us
  matrix products: 66.8 us -> 0 us
  local copies, waits for them, and re-layouts: 65.6 us -> 5.19 us
  between operations: 14.1 us -> 0.64 us
    all_to_all x40 -> x0, waiting for transfers between devices: 280 us -> none  [the longest x10 103 us: step_fn(): lax.all_to_all(summed_u.astype(jnp.bfloat16), 'expert', split_axis=0, con...]
    pallas_call x0 -> x1, Pallas kernels: none -> 234 us  [per_device(): pl.pallas_call(functools.partial(kernel, scale=scale), out_shape=(jax.Sha...]
    reduce_scatter x20 -> x0, waiting for transfers between devices: 209 us -> none  [the longest x10 166 us: step_fn(): lax.psum_scatter(gate_part, 'dp', scatter_dimension=0, tiled=True)]
    all_to_all x40 -> x0, starting transfers between devices: 202 us -> none  [the longest x10 64 us: step_fn(): lax.all_to_all(summed_u.astype(jnp.bfloat16), 'expert', split_axis=0, con...]
    psum x1 -> x0, blocking collectives: 121 us -> none  [per_device(): lax.psum(final_state[2].astype(jnp.bfloat16), ('expert', 'dp'))]
    all_gather x20 -> x0, blocking collectives: 120 us -> none  [the longest x10 64.3 us: step_fn(): lax.all_gather(recv_grad, 'dp', axis=0, tiled=True)]
    dot_general x69 -> x0, matrix products: 66.8 us -> none  [the longest x3 15.7 us: expert_terms(): lax.dot_general(rows_grad, second_proj, (((1,), (1,)), ((), ())), preferr...]
    ppermute x10 -> x0, waiting for transfers between devices: 44 us -> none  [from_behind(): return lax.ppermute(shard, axis, pairs)]
  transfers between devices with their start and end apart: 70 -> 0, of which waited for: 70 -> 0; matrix products, arithmetic and copies ran while one was open for 5% -> 0% of each run, Pallas kernels for 0% -> 0%
where the time goes in v1:
time: 243 us
  Pallas kernels  234 us (96%)
  local copies, waits for them, and re-layouts  5.19 us (2%)
  other arithmetic  2.9 us (1%)
    pallas_call x1, Pallas kernels, per_device(): pl.pallas_call(functools.partial(kernel, scale=scale), out_shape=(jax.Sha...  234 us
    unnamed x4, local copies, waits for them, and re-layouts  5.19 us

profile of v1, /device:TPU:1, one launch (start us, length us, event | category | flops | bytes accessed | tf_op | source)
XLA Modules:
  0.0 243.1 jit_solution(15904073400470684523)
XLA Ops:
  0.6 0.7 copy.14
  1.3 0.8 select_reduce_fusion
  2.1 0.7 compare_select_fusion
  2.8 1.4 pad_add_fusion
  4.2 234.3 %shard_map.112 = (bf16[3,64,1024]{2,1,0:T(8,128)(2,1)}, f32[1,1024]{1,0:T(1,128)}, f32[16,1024]{1,0:T(8,128)}) custom-call(bf16[3,64,1024]{2,1,0:T(8,128)(2,1)} %bitcast.26, bf16[3,64,1024]{2,1,0:T(8,128)(2,1)} %out_grad.1, f32[1,1024]{1,0:T(1,128)} %gain.1, bf16[16,1024]{1,0:T(8,128)(2,1)} %bitcast.29, s32[3,2,128]{2,1,0:T(2,128)} %get-tuple-element.9.ids, ...), custom_call_target="tpu_custom_call" | custom-call | tf_op jit(solution)/shard_map/pallas_call | solution.py:440
  238.6 1.8 copy.18
  240.3 1.3 copy.19
  241.6 1.5 copy.20

commit v2 on v1

v2 whole, which is shorter than its diff:
```python
import functools
import math

import jax
import jax.numpy as jnp
from jax import lax
from jax.experimental import pallas as pl
from jax.experimental.pallas import tpu as pltpu
from jax.sharding import PartitionSpec as P

GELU_C = math.sqrt(2.0 / math.pi)
MESH = pl.DeviceIdType.MESH
BF = jnp.bfloat16
F32 = jnp.float32
SIDE = 4
LANES = 128


def plane_offsets():
    offs = [(k // SIDE, k % SIDE) for k in range(1, SIDE * SIDE)]
    far = lambda o: min(o[0], SIDE - o[0]) + min(o[1], SIDE - o[1])
    return sorted(offs, key=lambda o: -far(o))


def dot(a, b, ca=1, cb=0):
    return lax.dot_general(a, b, (((ca,), (cb,)), ((), ())), preferred_element_type=F32)


def iota(shape, dim):
    return lax.broadcasted_iota(jnp.int32, shape, dim)


def stack_chunks(x):
    return jnp.concatenate([x[:, c : c + LANES] for c in range(0, x.shape[1], LANES)], axis=0)


def spread_chunks(x, rows):
    return jnp.concatenate([x[r : r + rows] for r in range(0, x.shape[0], rows)], axis=1)


def kernel(
    acts, out_grad, gain, router_t, ids, places, caps, w_in_own, w_out_own,
    o_grads, o_gain, o_router,
    w_in, w_out, w_out_t, slope, active, pre, rows, back_s,
    su, ru, sg, rg, sy, ry, sr, rr, rz, sz,
    unit_s, inv_s, normed_s, ydiff_s, extra_s, pdg_s,
    send_main, send_tail, mix_main, mix_tail, diff_main, diff_tail,
    router_pad, perm, perm_t, eye, router_acc, gain_acc,
    fin_s, fin_r, fin_x, fin_y, fin_t, fin_g, gain_x, gain_y, gain_t, gain_g,
    w_local, w_send, w_recv,
    u_send, u_recv, g_send, g_recv, z_send, z_recv, y_send, y_recv, r_send, r_recv,
    f_send, f_recv,
    *, scale,
):
    sec = lax.axis_index("section")
    exp = lax.axis_index("expert")
    core = lax.axis_index("dp")
    sections = lax.axis_size("section")
    last = sections - 1
    col = exp // SIDE
    row = lax.rem(exp, SIDE)
    peers = [
        lax.rem(col + dy, SIDE) * SIDE + lax.rem(row + dx, SIDE) for dy, dx in plane_offsets()
    ]
    experts = SIDE * SIDE
    micros = acts.shape[0]
    toks = acts.shape[1]
    width = acts.shape[2]
    half = w_in_own.shape[1]

    own_in = pltpu.make_async_copy(w_in_own, w_in.at[:, pl.ds(0, half)], w_local.at[0])
    own_out = pltpu.make_async_copy(w_out_own, w_out.at[pl.ds(0, half), :], w_local.at[1])
    own_in.start()
    own_out.start()

    barrier = pltpu.get_barrier_semaphore()
    for p in peers:
        pl.semaphore_signal(barrier, inc=1, device_id=(sec, p, core), device_id_type=MESH)
    pl.semaphore_signal(barrier, inc=1, device_id=(sec, exp, 1 - core), device_id_type=MESH)

    @pl.when(sec < last)
    def _():
        pl.semaphore_signal(barrier, inc=1, device_id=(sec + 1, exp, core), device_id_type=MESH)

    part_in = pltpu.make_async_remote_copy(
        src_ref=w_in_own, dst_ref=w_in.at[:, pl.ds(half, half)],
        send_sem=w_send.at[0], recv_sem=w_recv.at[0],
        device_id=(sec, exp, 1 - core), device_id_type=MESH,
    )
    part_out = pltpu.make_async_remote_copy(
        src_ref=w_out_own, dst_ref=w_out.at[pl.ds(half, half), :],
        send_sem=w_send.at[1], recv_sem=w_recv.at[1],
        device_id=(sec, exp, 1 - core), device_id_type=MESH,
    )

    def scatter(src_of, dst_of, send_sem, recv_sem):
        for p in peers:
            pltpu.make_async_remote_copy(
                src_ref=src_of(p), dst_ref=dst_of(exp), send_sem=send_sem, recv_sem=recv_sem,
                device_id=(sec, p, core), device_id_type=MESH,
            ).start()

    def others(part, sem):
        return pltpu.make_async_copy(part, part, sem)

    def all_parts(buf, m, h, sem):
        return others(buf.at[m, h, pl.ds(0, experts - 1)], sem.at[m, h])

    def all_rows(buf, m, sem):
        return others(buf.at[m, pl.ds(0, experts - 1)], sem.at[m])

    def send_part(src, dst, m, h, send_sem, recv_sem):
        scatter(
            lambda p: src.at[m, h, p], lambda p: dst.at[m, h, p],
            send_sem.at[m, h], recv_sem.at[m, h],
        )
        dst[m, h, exp] = src[m, h, exp]

    def send_rows(src, dst, m, lines, send_sem, recv_sem):
        scatter(
            lambda p: src.at[m, p, lines], lambda p: dst.at[m, p, lines],
            send_sem.at[m], recv_sem.at[m],
        )
        dst[m, exp, lines] = src[m, exp, lines]

    def two_tiles(main):
        main = main.reshape(experts, 8, 4 * LANES)
        return [
            jnp.concatenate([main[:, :, c : c + LANES], main[:, :, c + LANES : c + 2 * LANES]], axis=1).astype(BF)
            for c in (0, 2 * LANES)
        ]

    def from_tiles(tiles):
        parts = []
        for t in tiles:
            t = t.astype(F32)
            parts.append(t[:, :8, :].reshape(experts * 8, LANES))
            parts.append(t[:, 8:, :].reshape(experts * 8, LANES))
        return jnp.concatenate(parts, axis=1).astype(BF)

    def to_slots(x, m, h, buf):
        tiles = two_tiles(dot(send_main[m], x))
        buf[m, h, :, 0:16, :] = tiles[0]
        buf[m, h, :, 16:32, :] = tiles[1]
        tail = dot(send_tail[m], stack_chunks(x))
        buf[m, h, :, 32:48, :] = tail.reshape(experts, 16, LANES).astype(BF)

    def to_rows(buf, m, h):
        cols = slice(512 * h, 512 * h + 512)
        rows[0 : experts * 8, cols] = from_tiles([buf[m, h, :, 0:16, :], buf[m, h, :, 16:32, :]])
        t = dot(perm[...], buf[m, h, :, 32:48, :].reshape(experts * 16, LANES))
        rows[experts * 8 : experts * 10, cols] = spread_chunks(t, experts * 2).astype(BF)

    def from_rows(product, m, buf, dst, send_sem, recv_sem):
        tails = []
        for h in range(2):
            res = product(slice(512 * h, 512 * h + 512))
            tiles = two_tiles(res[0 : experts * 8])
            buf[m, :, 32 * h : 32 * h + 16, :] = tiles[0]
            buf[m, :, 32 * h + 16 : 32 * h + 32, :] = tiles[1]
            tails.append(stack_chunks(res[experts * 8 : experts * 10].astype(BF)))
            if h == 0:
                send_rows(buf, dst, m, pl.ds(0, 32), send_sem, recv_sem)
        tail = dot(perm_t[...], jnp.concatenate(tails, axis=0))
        buf[m, :, 64:80, :] = tail.reshape(experts, 16, LANES).astype(BF)
        send_rows(buf, dst, m, pl.ds(32, 48), send_sem, recv_sem)

    def combine(buf, m, main_table, tail_table):
        tiles = [buf[m, :, 16 * q : 16 * q + 16, :] for q in range(4)]
        main = dot(main_table[m], from_tiles(tiles))
        tail = dot(tail_table[m], buf[m, :, 64:80, :].reshape(experts * 16, LANES))
        return main + spread_chunks(tail, toks)

    def grad_of(m):
        return jnp.concatenate([rz[m, 0], rz[m, 1]], axis=1)

    q = iota((256, 256), 0)
    r = iota((256, 256), 1)
    q_half = iota((128, 256), 0)
    picked = ((q_half & 31) >> 1) * 16 + (q_half & 1) * 4 + (q_half >> 5)
    perm[...] = (iota((128, 256), 1) == picked).astype(F32).astype(BF)
    picked_t = ((r & 31) >> 1) * 16 + (r & 1) * 8 + (r >> 5)
    perm_t[...] = (q == picked_t).astype(F32).astype(BF)
    eye[...] = (q == r).astype(F32).astype(BF)
    router_pad[...] = jnp.zeros_like(router_pad)
    router_pad[0:experts, :] = router_t[...]
    router_acc[...] = jnp.zeros_like(router_acc)
    gain_acc[...] = jnp.zeros_like(gain_acc)

    e_r = iota((experts, LANES), 0)

    def twice(line):
        return jnp.concatenate([line, line], axis=1)

    def code_lines(m):
        square = iota((experts, experts), 0) == iota((experts, experts), 1)
        limit = jnp.sum(jnp.where(square, caps[m].astype(F32), 0.0), axis=1, keepdims=True)
        found = []
        for k in range(2):
            chosen = twice(ids[m, k : k + 1, :])
            place = twice(places[m, k : k + 1, :])
            most = jnp.sum(jnp.where(e_r == chosen, limit, 0.0), axis=0, keepdims=True)
            found += [chosen, jnp.where(place.astype(F32) < most, chosen * 16 + place, -1)]
        return found

    def tokens_forward(m):
        x = acts[m].astype(F32)
        centred = x - jnp.mean(x, axis=-1, keepdims=True)
        inv = lax.rsqrt(jnp.mean(centred * centred, axis=-1, keepdims=True) + 1e-06)
        unit = centred * inv
        normed = (unit * gain[...]).astype(BF)
        unit_s[m] = unit
        inv_s[m] = jnp.broadcast_to(inv, (toks, LANES))
        normed_s[m] = normed
        _, code1, _, code2 = code_lines(m)
        slot_r = iota((128, LANES), 0)
        slot_code = (slot_r >> 3) * 16 + (slot_r & 7)
        hit = ((slot_code == code1) | (slot_code == code2)).astype(F32)
        send_main[m] = hit[:, :toks].astype(BF)
        wide1 = jnp.concatenate([code1] * 2, axis=1)
        wide2 = jnp.concatenate([code2] * 2, axis=1)
        tail_r = iota((256, 256), 0)
        tail_code = (tail_r >> 4) * 16 + 8 + ((tail_r >> 2) & 1)
        same = ((iota((256, 256), 1) >> 6) == (tail_r & 3)) & ((tail_r & 8) == 0)
        hit = (((tail_code == wide1) | (tail_code == wide2)) & same).astype(F32)
        send_tail[m] = hit.astype(BF)
        for h in range(2):
            to_slots(normed[:, 512 * h : 512 * h + 512], m, h, su)

    def tokens_tables(m):
        id1, code1, id2, code2 = code_lines(m)
        normed = normed_s[m]
        logits = dot(router_t[...], jnp.concatenate([normed, normed], axis=0), 1, 1)
        chosen1 = jnp.sum(jnp.where(e_r == id1, logits, 0.0), axis=0, keepdims=True)
        chosen2 = jnp.sum(jnp.where(e_r == id2, logits, 0.0), axis=0, keepdims=True)
        gate1 = 1.0 / (1.0 + jnp.exp(chosen2 - chosen1))
        gate2 = 1.0 - gate1
        line = iota((8, LANES), 0)
        lines = jnp.where(line == 0, code1.astype(F32), 0.0)
        lines = jnp.where(line == 1, code2.astype(F32), lines)
        lines = jnp.where(line == 2, id1.astype(F32), lines)
        lines = jnp.where(line == 3, id2.astype(F32), lines)
        lines = jnp.where(line == 4, gate1, lines)
        lines = jnp.where(line == 5, gate2, lines)
        lines = jnp.concatenate([lines, jnp.zeros((LANES - 8, LANES), F32)], axis=0)
        turned = jnp.transpose(lines)[:toks]
        c1 = turned[:, 0:1].astype(jnp.int32)
        c2 = turned[:, 1:2].astype(jnp.int32)
        i1 = turned[:, 2:3].astype(jnp.int32)
        i2 = turned[:, 3:4].astype(jnp.int32)
        g1 = turned[:, 4:5]
        g2 = turned[:, 5:6]
        e_l = iota((toks, LANES), 1)
        pdg_s[m] = g1 * g2 * ((e_l == i1).astype(F32) - (e_l == i2).astype(F32))
        slot_code = (e_l >> 3) * 16 + (e_l & 7)
        hit1 = (slot_code == c1).astype(F32)
        hit2 = (slot_code == c2).astype(F32)
        mix_main[m] = (g1 * hit1 + g2 * hit2).astype(BF)
        diff_main[m] = (hit1 - hit2).astype(BF)
        lane = iota((toks, 256), 1)
        tail_code = (lane >> 4) * 16 + 8 + ((lane >> 3) & 1)
        hit1 = (tail_code == c1).astype(F32)
        hit2 = (tail_code == c2).astype(F32)
        mixed = g1 * hit1 + g2 * hit2
        differ = hit1 - hit2
        for c in range(8):
            here = (lane & 7) == c
            mix_tail[m, toks * c : toks * c + toks, :] = jnp.where(here, mixed, 0.0).astype(BF)
            diff_tail[m, toks * c : toks * c + toks, :] = jnp.where(here, differ, 0.0).astype(BF)

    def experts_forward(m):
        for h in range(2):
            all_parts(ru, m, h, u_recv).wait()
            to_rows(ru, m, h)
        for n in range(4):
            cols = slice(1024 * n, 1024 * n + 1024)
            hidden = dot(rows[...], w_in[:, cols])
            square = hidden * hidden
            tanh = jnp.tanh(GELU_C * hidden * (1.0 + 0.044715 * square))
            rise = 0.5 * (1.0 + tanh)
            active[m, :, cols] = (hidden * rise).astype(BF)
            bend = 0.5 * hidden * (1.0 - tanh * tanh) * (GELU_C + (3.0 * 0.044715 * GELU_C) * square)
            slope[m, :, cols] = (rise + bend).astype(BF)

    def experts_value(m):
        from_rows(lambda cols: dot(active[m], w_out[:, cols]), m, sy, ry, y_send, y_recv)

    def tokens_value(m):
        all_rows(ry, m, y_recv).wait()
        ydiff_s[m] = combine(ry, m, diff_main, diff_tail)

    def tokens_send(m, h):
        to_slots(rz[m, h], m, h, sg)
        send_part(sg, rg, m, h, g_send, g_recv)

    def tokens_gate(m):
        dots = jnp.sum(ydiff_s[m] * grad_of(m).astype(F32), axis=1, keepdims=True)
        dlogits = (dots * pdg_s[m]).astype(BF)
        extra_s[m] = dot(dlogits, router_pad[...])
        router_acc[...] += dot(dlogits, normed_s[m], 0, 0)[:experts]

    def experts_backward(m, turned):
        def product(h):
            cols = slice(512 * h, 512 * h + 512)
            if turned:
                return dot(rows[:, cols], w_out_t[cols, :])
            return dot(rows[:, cols], w_out[:, cols], 1, 1)

        all_parts(rg, m, 0, g_recv).wait()
        to_rows(rg, m, 0)
        back_s[...] = product(0)
        all_parts(rg, m, 1, g_recv).wait()
        to_rows(rg, m, 1)
        pre[...] = ((back_s[...] + product(1)) * slope[m].astype(F32)).astype(BF)

    def experts_return(m, turned):
        def product(cols):
            if turned:
                return dot(pre[...], w_out[:, cols])
            return dot(pre[...], w_in[cols, :], 1, 1)

        from_rows(product, m, sr, rr, r_send, r_recv)

    def tokens_backward(m):
        all_rows(rr, m, r_recv).wait()
        unit = unit_s[m]
        norm_grad = combine(rr, m, mix_main, mix_tail) + extra_s[m]
        xhat = norm_grad * gain[...]
        mean1 = jnp.mean(xhat, axis=-1, keepdims=True)
        mean2 = jnp.mean(xhat * unit, axis=-1, keepdims=True)
        step = inv_s[m][:, 0:1] * (xhat - mean1 - unit * mean2)
        in_grad = (grad_of(m).astype(F32) + step).astype(BF)
        for h in range(2):
            sz[m, h] = in_grad[:, 512 * h : 512 * h + 512]

            @pl.when(sec > 0)
            def _():
                z_copy(m, h).start()

        o_grads[m] = in_grad
        terms = (norm_grad * unit).reshape(toks // 8, 8, width)
        gain_acc[...] += jnp.sum(terms, axis=0)

    def z_copy(m, h):
        return pltpu.make_async_remote_copy(
            src_ref=sz.at[m, h], dst_ref=rz.at[m, h],
            send_sem=z_send.at[m, h], recv_sem=z_recv.at[m, h],
            device_id=(jnp.maximum(sec - 1, 0), exp, core), device_id_type=MESH,
        )

    def tile(j):
        lines = slice(8 * (j // 8), 8 * (j // 8) + 8)
        return lines, slice(LANES * (j % 8), LANES * (j % 8) + LANES)

    def to_peers(src_of, dst, k):
        scatter(src_of, lambda p: dst.at[p], f_send.at[k], f_recv.at[k])

    def to_pair(src, dst, k):
        return pltpu.make_async_remote_copy(
            src_ref=src, dst_ref=dst, send_sem=f_send.at[k], recv_sem=f_recv.at[k],
            device_id=(sec, exp, 1 - core), device_id_type=MESH,
        )

    def all_but_one(buf, sem, k):
        return others(buf.at[pl.ds(0, experts - 1)], sem.at[k])

    def router_parts():
        for j in range(experts):
            lines, cols = tile(j)
            fin_s[j] = router_acc[lines, cols]
        to_peers(lambda p: fin_s.at[p], fin_r, 0)
        fin_r[exp] = fin_s[exp]

    def router_sums():
        all_but_one(fin_r, f_recv, 0).wait()
        fin_x[...] = jnp.sum(fin_r[...], axis=0)
        pair = to_pair(fin_x, fin_y, 1)
        pair.start()
        pair.wait()
        fin_t[...] = (fin_x[...] + fin_y[...]) * scale
        to_peers(lambda p: fin_t, fin_g, 2)
        fin_g[exp] = fin_t[...]

    def gain_sums():
        gain_x[...] = jnp.sum(gain_acc[...], axis=0, keepdims=True)
        pair = to_pair(gain_x, gain_y, 3)
        pair.start()
        pair.wait()
        gain_t[...] = (gain_x[...] + gain_y[...]) * scale
        to_peers(lambda p: gain_t, gain_g, 4)
        gain_g[exp] = gain_t[...]

    tokens_forward(0)

    @pl.when(sec == last)
    def _():
        for m in range(micros):
            for h in range(2):
                rz[m, h] = out_grad[m, :, 512 * h : 512 * h + 512]
        for h in range(2):
            to_slots(rz[0, h], 0, h, sg)

    @pl.when(sec > 0)
    def _():
        pl.semaphore_wait(barrier, experts + 1)

    @pl.when(sec == 0)
    def _():
        pl.semaphore_wait(barrier, experts)

    part_in.start()
    for h in range(2):
        send_part(su, ru, 0, h, u_send, u_recv)

    @pl.when(sec == last)
    def _():
        for h in range(2):
            send_part(sg, rg, 0, h, g_send, g_recv)

    tokens_tables(0)

    @pl.loop(1, micros)
    def _(m):
        tokens_forward(m)
        for h in range(2):
            send_part(su, ru, m, h, u_send, u_recv)

        @pl.when(sec == last)
        def _():
            for h in range(2):
                tokens_send(m, h)

        tokens_tables(m)

    part_out.start()
    own_in.wait()
    part_in.wait_recv()
    pl.loop(0, micros)(experts_forward)
    own_out.wait()
    part_out.wait_recv()
    experts_value(0)

    @pl.when(sec == last)
    def _():
        experts_backward(0, False)
        experts_return(0, False)
        experts_value(1)
        tokens_value(0)
        tokens_gate(0)
        experts_backward(1, False)
        tokens_backward(0)
        experts_return(1, False)
        experts_value(2)
        tokens_value(1)
        tokens_gate(1)
        experts_backward(2, False)
        tokens_backward(1)
        experts_return(2, False)
        tokens_value(2)
        tokens_gate(2)
        router_parts()

    @pl.when(sec < last)
    def _():
        pl.loop(1, micros)(experts_value)

        @pl.loop(0, width // 256)
        def _(n):
            lines = pl.ds(pl.multiple_of(n * 256, 256), 256)
            w_out_t[lines, :] = dot(eye[...], w_out[:, lines], 1, 1).astype(BF)

        @pl.loop(0, 2 * half // 256)
        def _(n):
            lines = pl.ds(pl.multiple_of(n * 256, 256), 256)
            w_out[lines, :] = dot(eye[...], w_in[:, lines], 1, 1).astype(BF)

        pl.loop(0, micros)(tokens_value)

        @pl.loop(0, micros)
        def _(m):
            for h in range(2):
                z_copy(m, h).wait_recv()
                tokens_send(m, h)
            tokens_gate(m)

            @pl.when(m > 0)
            def _():
                tokens_backward(m - 1)

            @pl.when(m == micros - 1)
            def _():
                router_parts()

            experts_backward(m, True)
            experts_return(m, True)

    router_sums()
    tokens_backward(micros - 1)
    gain_sums()
    all_but_one(fin_g, f_recv, 2).wait()
    for j in range(experts):
        lines, cols = tile(j)
        o_router[lines, cols] = fin_g[j]
    all_but_one(gain_g, f_recv, 4).wait()
    o_gain[...] = jnp.sum(gain_g[...], axis=0)

    @pl.loop(0, micros)
    def _(m):
        all_rows(sy, m, y_send).wait()
        all_rows(sr, m, r_send).wait()
        for h in range(2):
            all_parts(su, m, h, u_send).wait()
            all_parts(sg, m, h, g_send).wait()

            @pl.when(sec > 0)
            def _():
                z_copy(m, h).wait_send()

    all_but_one(fin_r, f_send, 0).wait()
    all_but_one(fin_g, f_send, 2).wait()
    all_but_one(gain_g, f_send, 4).wait()
    part_in.wait_send()
    part_out.wait_send()


def copy_out(a, b, c, to_a, to_b, to_c):
    to_a[...] = a[...]
    to_b[...] = b[...]
    to_c[...] = c[...]


def per_device(acts, out_grad, ln_gain, router, w_in, w_out, expert_ids, slot_ids, capacity):
    _, micros, toks, width = acts.shape
    experts = router.shape[2]
    half = w_in.shape[3]
    cap_slots = 10
    slots = experts * cap_slots
    tokens_all = toks * lax.axis_size("expert") * lax.axis_size("dp")
    scale = 1.0 / math.sqrt(micros * tokens_all)
    ids = jnp.transpose(expert_ids[0], (0, 2, 1))
    places = jnp.transpose(slot_ids[0], (0, 2, 1))
    caps = jnp.transpose(capacity, (1, 0, 2))
    vmem = pl.BlockSpec(memory_space=pltpu.VMEM)
    hbm = pl.BlockSpec(memory_space=pl.ANY)
    dma = pltpu.SemaphoreType.DMA
    grads, gain_out, router_out = pl.pallas_call(
        functools.partial(kernel, scale=scale),
        out_shape=(
            jax.ShapeDtypeStruct((micros, toks, width), BF),
            jax.ShapeDtypeStruct((1, width), F32),
            jax.ShapeDtypeStruct((experts, width), F32),
        ),
        in_specs=[vmem] * 7 + [hbm] * 2,
        out_specs=(vmem, vmem, vmem),
        scratch_shapes=[
            pltpu.VMEM((width, 2 * half), BF),
            pltpu.VMEM((2 * half, width), BF),
            pltpu.VMEM((width, 2 * half), BF),
            pltpu.VMEM((micros, slots, 2 * half), BF),
            pltpu.VMEM((micros, slots, 2 * half), BF),
            pltpu.VMEM((slots, 2 * half), BF),
            pltpu.VMEM((slots, width), BF),
            pltpu.VMEM((slots, 2 * half), F32),
        ]
        + [pltpu.VMEM((micros, 2, experts, 48, LANES), BF)] * 4
        + [pltpu.VMEM((micros, experts, 80, LANES), BF)] * 4
        + [pltpu.VMEM((micros, 2, toks, width // 2), BF)] * 2
        + [
            pltpu.VMEM((micros, toks, width), F32),
            pltpu.VMEM((micros, toks, LANES), F32),
            pltpu.VMEM((micros, toks, width), BF),
            pltpu.VMEM((micros, toks, width), F32),
            pltpu.VMEM((micros, toks, width), F32),
            pltpu.VMEM((micros, toks, LANES), F32),
            pltpu.VMEM((micros, 128, toks), BF),
            pltpu.VMEM((micros, 256, 256), BF),
            pltpu.VMEM((micros, toks, 128), BF),
            pltpu.VMEM((micros, 512, 256), BF),
            pltpu.VMEM((micros, toks, 128), BF),
            pltpu.VMEM((micros, 512, 256), BF),
            pltpu.VMEM((LANES, width), BF),
            pltpu.VMEM((128, 256), BF),
            pltpu.VMEM((256, 256), BF),
            pltpu.VMEM((256, 256), BF),
            pltpu.VMEM((experts, width), F32),
            pltpu.VMEM((8, width), F32),
            pltpu.VMEM((experts, 8, LANES), F32),
            pltpu.VMEM((experts, 8, LANES), F32),
            pltpu.VMEM((8, LANES), F32),
            pltpu.VMEM((8, LANES), F32),
            pltpu.VMEM((8, LANES), F32),
            pltpu.VMEM((experts, 8, LANES), F32),
            pltpu.VMEM((1, width), F32),
            pltpu.VMEM((1, width), F32),
            pltpu.VMEM((1, width), F32),
            pltpu.VMEM((experts, 1, width), F32),
            dma((2,)),
            dma((2,)),
            dma((2,)),
        ]
        + [dma((micros, 2))] * 6
        + [dma((micros,))] * 4
        + [dma((5,))] * 2,
        compiler_params=pltpu.CompilerParams(
            collective_id=0, has_side_effects=True, vmem_limit_bytes=60 * 2**20
        ),
    )(
        acts[0],
        out_grad,
        ln_gain,
        jnp.transpose(router[0]),
        ids,
        places,
        caps,
        w_in[0, 0],
        w_out[0, 0],
    )
    grads, gain_out, router_out = pl.pallas_call(
        copy_out,
        out_shape=(
            jax.ShapeDtypeStruct((micros, toks, width), BF),
            jax.ShapeDtypeStruct((1, width), F32),
            jax.ShapeDtypeStruct((experts, width), F32),
        ),
        in_specs=[vmem] * 3,
        out_specs=(vmem, vmem, vmem),
    )(grads, gain_out, router_out)
    return (grads[None], gain_out, jnp.transpose(router_out)[None])


def solution(mesh):
    return jax.shard_map(
        per_device,
        mesh=mesh,
        in_specs=(
            P("section", None, ("expert", "dp"), None),
            P(None, ("expert", "dp"), None),
            P("section", None),
            P("section", None, None),
            P("section", "expert", None, "dp"),
            P("section", "expert", "dp", None),
            P("section", None, ("expert", "dp"), None),
            P("section", None, ("expert", "dp"), None),
            P("section", None, None),
        ),
        out_specs=(
            P("section", None, ("expert", "dp"), None),
            P("section", None),
            P("section", None, None),
        ),
        check_vma=False,
    )
```

time: 243 us -> 214 us (0.88)
  Pallas kernels: 234 us -> 213 us
  local copies, waits for them, and re-layouts: 5.19 us -> 0 us
  other arithmetic: 2.9 us -> 0 us
    pallas_call x1, Pallas kernels: 234 us -> 212 us  [per_device(): pl.pallas_call(functools.partial(kernel, scale=scale), out_shape=(jax.Sha...]
    unnamed x4 -> x0, local copies, waits for them, and re-layouts: 5.19 us -> none
where the time goes in v2:
time: 214 us
  Pallas kernels  213 us (100%)
    pallas_call x1, Pallas kernels, per_device(): pl.pallas_call(functools.partial(kernel, scale=scale), out_shape=(jax.Sha...  212 us

profile of v2, /device:TPU:1, one launch (start us, length us, event | category | flops | bytes accessed | tf_op | source)
XLA Modules:
  0.0 214.0 jit_solution(13355457060980935821)
XLA Ops:
  0.6 211.5 %shard_map.112 = (bf16[3,64,1024]{2,1,0:T(8,128)(2,1)}, f32[1,1024]{1,0:T(1,128)}, f32[16,1024]{1,0:T(8,128)}) custom-call(bf16[3,64,1024]{2,1,0:T(8,128)(2,1)} %bitcast.19, bf16[3,64,1024]{2,1,0:T(8,128)(2,1)} %out_grad.1, f32[1,1024]{1,0:T(1,128)} %gain.1, bf16[16,1024]{1,0:T(8,128)(2,1)} %bitcast.20, s32[3,2,64]{2,1,0:T(2,128)} %bitcast.21, ...), custom_call_target="tpu_custom_call" | custom-call | tf_op jit(solution)/shard_map/pallas_call | solution.py:546
  212.2 1.8 shard_map.113

commit v3 on v2

--- a/solution.py
+++ b/solution.py
@@ -371,24 +371,22 @@
         to_peers(lambda p: fin_s.at[p], fin_r, 0)
         fin_r[exp] = fin_s[exp]
 
-    def router_sums():
+    def last_sums():
+        gain_x[...] = jnp.sum(gain_acc[...], axis=0, keepdims=True)
+        gain_pair = to_pair(gain_x, gain_y, 3)
+        gain_pair.start()
         all_but_one(fin_r, f_recv, 0).wait()
         fin_x[...] = jnp.sum(fin_r[...], axis=0)
         pair = to_pair(fin_x, fin_y, 1)
         pair.start()
+        gain_pair.wait()
+        gain_t[...] = (gain_x[...] + gain_y[...]) * scale
+        to_peers(lambda p: gain_t, gain_g, 4)
+        gain_g[exp] = gain_t[...]
         pair.wait()
         fin_t[...] = (fin_x[...] + fin_y[...]) * scale
         to_peers(lambda p: fin_t, fin_g, 2)
         fin_g[exp] = fin_t[...]
-
-    def gain_sums():
-        gain_x[...] = jnp.sum(gain_acc[...], axis=0, keepdims=True)
-        pair = to_pair(gain_x, gain_y, 3)
-        pair.start()
-        pair.wait()
-        gain_t[...] = (gain_x[...] + gain_y[...]) * scale
-        to_peers(lambda p: gain_t, gain_g, 4)
-        gain_g[exp] = gain_t[...]
 
     tokens_forward(0)
 
@@ -409,6 +407,7 @@
         pl.semaphore_wait(barrier, experts)
 
     part_in.start()
+    part_out.start()
     for h in range(2):
         send_part(su, ru, 0, h, u_send, u_recv)
 
@@ -432,37 +431,38 @@
 
         tokens_tables(m)
 
-    part_out.start()
     own_in.wait()
     part_in.wait_recv()
     pl.loop(0, micros)(experts_forward)
     own_out.wait()
     part_out.wait_recv()
-    experts_value(0)
 
     @pl.when(sec == last)
     def _():
-        experts_backward(0, False)
-        experts_return(0, False)
-        experts_value(1)
-        tokens_value(0)
-        tokens_gate(0)
-        experts_backward(1, False)
-        tokens_backward(0)
-        experts_return(1, False)
-        experts_value(2)
-        tokens_value(1)
-        tokens_gate(1)
-        experts_backward(2, False)
-        tokens_backward(1)
-        experts_return(2, False)
-        tokens_value(2)
-        tokens_gate(2)
+        @pl.loop(0, micros)
+        def _(m):
+            experts_value(m)
+
+            @pl.when(m > 0)
+            def _():
+                tokens_value(m - 1)
+                tokens_gate(m - 1)
+
+            experts_backward(m, False)
+
+            @pl.when(m > 0)
+            def _():
+                tokens_backward(m - 1)
+
+            experts_return(m, False)
+
+        tokens_value(micros - 1)
+        tokens_gate(micros - 1)
         router_parts()
 
     @pl.when(sec < last)
     def _():
-        pl.loop(1, micros)(experts_value)
+        pl.loop(0, micros)(experts_value)
 
         @pl.loop(0, width // 256)
         def _(n):
@@ -487,16 +487,13 @@
             def _():
                 tokens_backward(m - 1)
 
-            @pl.when(m == micros - 1)
-            def _():
-                router_parts()
-
             experts_backward(m, True)
             experts_return(m, True)
 
-    router_sums()
+        router_parts()
+
     tokens_backward(micros - 1)
-    gain_sums()
+    last_sums()
     all_but_one(fin_g, f_recv, 2).wait()
     for j in range(experts):
         lines, cols = tile(j)

time: 214 us -> 218 us (1.019)
  Pallas kernels: 213 us -> 217 us
    pallas_call x1, Pallas kernels: 212 us -> 215 us  [per_device(): pl.pallas_call(functools.partial(kernel, scale=scale), out_shape=(jax.Sha...]
where the time goes in v3:
time: 218 us
  Pallas kernels  217 us (100%)
    pallas_call x1, Pallas kernels, per_device(): pl.pallas_call(functools.partial(kernel, scale=scale), out_shape=(jax.Sha...  215 us

profile of v3, /device:TPU:1, one launch (start us, length us, event | category | flops | bytes accessed | tf_op | source)
XLA Modules:
  0.0 217.8 jit_solution(8956151753460088181)
XLA Ops:
  0.6 215.4 %shard_map.112 = (bf16[3,64,1024]{2,1,0:T(8,128)(2,1)}, f32[1,1024]{1,0:T(1,128)}, f32[16,1024]{1,0:T(8,128)}) custom-call(bf16[3,64,1024]{2,1,0:T(8,128)(2,1)} %bitcast.19, bf16[3,64,1024]{2,1,0:T(8,128)(2,1)} %out_grad.1, f32[1,1024]{1,0:T(1,128)} %gain.1, bf16[16,1024]{1,0:T(8,128)(2,1)} %bitcast.20, s32[3,2,64]{2,1,0:T(2,128)} %bitcast.21, ...), custom_call_target="tpu_custom_call" | custom-call | tf_op jit(solution)/shard_map/pallas_call | solution.py:543
  216.1 1.8 shard_map.113

commit v4 on v3

--- a/solution.py
+++ b/solution.py
@@ -371,22 +371,24 @@
         to_peers(lambda p: fin_s.at[p], fin_r, 0)
         fin_r[exp] = fin_s[exp]
 
-    def last_sums():
-        gain_x[...] = jnp.sum(gain_acc[...], axis=0, keepdims=True)
-        gain_pair = to_pair(gain_x, gain_y, 3)
-        gain_pair.start()
+    def router_sums():
         all_but_one(fin_r, f_recv, 0).wait()
         fin_x[...] = jnp.sum(fin_r[...], axis=0)
         pair = to_pair(fin_x, fin_y, 1)
         pair.start()
-        gain_pair.wait()
-        gain_t[...] = (gain_x[...] + gain_y[...]) * scale
-        to_peers(lambda p: gain_t, gain_g, 4)
-        gain_g[exp] = gain_t[...]
         pair.wait()
         fin_t[...] = (fin_x[...] + fin_y[...]) * scale
         to_peers(lambda p: fin_t, fin_g, 2)
         fin_g[exp] = fin_t[...]
+
+    def gain_sums():
+        gain_x[...] = jnp.sum(gain_acc[...], axis=0, keepdims=True)
+        pair = to_pair(gain_x, gain_y, 3)
+        pair.start()
+        pair.wait()
+        gain_t[...] = (gain_x[...] + gain_y[...]) * scale
+        to_peers(lambda p: gain_t, gain_g, 4)
+        gain_g[exp] = gain_t[...]
 
     tokens_forward(0)
 
@@ -458,7 +460,6 @@
 
         tokens_value(micros - 1)
         tokens_gate(micros - 1)
-        router_parts()
 
     @pl.when(sec < last)
     def _():
@@ -487,13 +488,25 @@
             def _():
                 tokens_backward(m - 1)
 
+            @pl.when((m == micros - 1) & (sec == 0))
+            def _():
+                router_parts()
+
             experts_backward(m, True)
             experts_return(m, True)
 
+    @pl.when(sec == 0)
+    def _():
+        router_sums()
+
+    tokens_backward(micros - 1)
+
+    @pl.when(sec > 0)
+    def _():
         router_parts()
-
-    tokens_backward(micros - 1)
-    last_sums()
+        router_sums()
+
+    gain_sums()
     all_but_one(fin_g, f_recv, 2).wait()
     for j in range(experts):
         lines, cols = tile(j)

time: 218 us -> 218 us (level)
  no operation moved by 1% of the time
where the time goes in v4:
time: 218 us; the launch traced here: 217 us
  Pallas kernels  217 us (100%)
    pallas_call x1, Pallas kernels, per_device(): pl.pallas_call(functools.partial(kernel, scale=scale), out_shape=(jax.Sha...  215 us

profile of v4, /device:TPU:1, one launch (start us, length us, event | category | flops | bytes accessed | tf_op | source)
XLA Modules:
  0.0 217.4 jit_solution(10343106427725270053)
XLA Ops:
  0.6 215.0 %shard_map.112 = (bf16[3,64,1024]{2,1,0:T(8,128)(2,1)}, f32[1,1024]{1,0:T(1,128)}, f32[16,1024]{1,0:T(8,128)}) custom-call(bf16[3,64,1024]{2,1,0:T(8,128)(2,1)} %bitcast.19, bf16[3,64,1024]{2,1,0:T(8,128)(2,1)} %out_grad.1, f32[1,1024]{1,0:T(1,128)} %gain.1, bf16[16,1024]{1,0:T(8,128)(2,1)} %bitcast.20, s32[3,2,64]{2,1,0:T(2,128)} %bitcast.21, ...), custom_call_target="tpu_custom_call" | custom-call | tf_op jit(solution)/shard_map/pallas_call | solution.py:556
  215.6 1.8 shard_map.113
